TPU v7x, 32 devices: a whole 2x2x4 slice. The times are simulated.
32 devices in a mesh: dp: 8 (over y, x, core), tp: 4 (over z).
Axes of the slice: x: 2, y: 2, z: 4, core: 2. Of those that a mesh axis runs over, the one named last changes fastest.
Arguments:
- tokens: bfloat16 [32768, 1024], P(('dp', 'tp')), may hold values from -6 to 6
- segment_ids: int32 [64, 512], P(('dp', 'tp')), may hold values from -1 to 7, as said below
- w_query: bfloat16 [1024, 1024], P(('dp', 'tp')), may hold values from -0.1875 to 0.1875
- w_key: bfloat16 [1024, 1024], P(('dp', 'tp')), may hold values from -0.1875 to 0.1875
- w_value: bfloat16 [1024, 1024], P(('dp', 'tp')), may hold values from -0.1875 to 0.1875
- w_output: bfloat16 [1024, 1024], P(('dp', 'tp')), may hold values from -1.5 to 1.5
- bias_query: float32 [1024], replicated, may hold values from -3 to 3
- bias_value: float32 [1024], replicated, may hold values from -3 to 3
- bias_output: float32 [1024], replicated, may hold values from -3 to 3
- gain_attn: float32 [1024], replicated, may hold values from 0.5 to 1.5
- beta_attn: float32 [1024], replicated, may hold values from -3 to 3
- w_inner: bfloat16 [1024, 4096], P(None, 'tp'), may hold values from -0.1875 to 0.1875
- bias_inner: float32 [4096], P('tp'), may hold values from -3 to 3
- w_outer: bfloat16 [4096, 1024], P('tp'), may hold values from -0.09375 to 0.09375
- bias_outer: float32 [1024], replicated, may hold values from -3 to 3
- gain_ffn: float32 [1024], replicated, may hold values from 0.5 to 1.5
- beta_ffn: float32 [1024], replicated, may hold values from -3 to 3
- cotangent: bfloat16 [32768, 1024], P(('dp', 'tp'))
Outputs:
- layer_out: bfloat16 [32768, 1024], P(('dp', 'tp'))
- tokens_grad: float32 [32768, 1024], P(('dp', 'tp'))
- grad_bias_query: float32 [1024], replicated
- grad_bias_value: float32 [1024], replicated
- grad_bias_output: float32 [1024], replicated
- grad_beta_attn: float32 [1024], replicated
- grad_bias_inner: float32 [4096], P('tp')
- grad_bias_outer: float32 [1024], replicated
- grad_beta_ffn: float32 [1024], replicated
Inputs may be any that keep to these rules, and one draw needn't show every extreme that they name: `segment_ids`: in each packed row of 512 slots the filled slots come first and carry their document's number within the row, starting at 0 and never falling; a row holds at most 8 documents; empty slots form the row's tail and carry -1; between 153 and 512 slots of a row are filled. Attention only joins slots of equal value.
All inputs are finite; a program needn't handle non-finite values.
Results may differ from a plain program's by a relative error of at most 0.015.
Values may be sent and summed in bfloat16 or wider, within the bound.
No kernel may reach another device: no remote copies, remote signals or barrier semaphores. Data moves between devices by JAX's collectives and lax.ppermute only.
A program may use at most 192 MiB of HBM per device.

v0:
```python
import jax
import jax.numpy as jnp
from jax import lax
from jax.sharding import PartitionSpec as P

HEADS = 16


norm_epsilon = 1e-12


def product(left, right):
    return jnp.dot(left, right, preferred_element_type=jnp.float32)


def layer_norm(resid, gain, beta):
    centered = resid - jnp.mean(resid, axis=-1, keepdims=True)
    spread = jnp.mean(centered * centered, axis=-1, keepdims=True)
    return centered * lax.rsqrt(spread + norm_epsilon) * gain + beta


def exact_gelu(value):
    return jax.nn.gelu(value, approximate=False)


def masked_scores(queries, key_rows, segments):
    scores = jnp.einsum(
        "qhd,khd->hqk", queries, key_rows, preferred_element_type=jnp.float32
    ) * queries.shape[-1] ** (-0.5)
    same_doc = (segments[:, None] == segments[None, :])[None]
    return jnp.where(same_doc, scores, -1000000000.0)


def attend(block):
    queries, key_rows, value_rows, segments = block
    scores = masked_scores(queries, key_rows, segments)
    log_total = jax.nn.logsumexp(scores, axis=-1)
    probs = jnp.exp(scores - log_total[..., None]).astype(jnp.bfloat16)
    mixed = jnp.einsum("hqk,khd->qhd", probs, value_rows, preferred_element_type=jnp.float32)
    return (mixed.astype(jnp.bfloat16), log_total)


def attend_back(block):
    queries, key_rows, value_rows, segments, out_grad, log_total = block
    scale = queries.shape[-1] ** (-0.5)
    probs = jnp.exp(masked_scores(queries, key_rows, segments) - log_total[..., None])
    prob_grad = jnp.einsum("qhd,khd->hqk", out_grad, value_rows, preferred_element_type=jnp.float32)
    value_grad = jnp.einsum(
        "hqk,qhd->khd", probs.astype(jnp.bfloat16), out_grad, preferred_element_type=jnp.float32
    )
    inner_sum = jnp.sum(prob_grad * probs, axis=-1, keepdims=True)
    score_grad = (probs * (prob_grad - inner_sum)).astype(jnp.bfloat16)
    query_grad = (
        jnp.einsum("hqk,khd->qhd", score_grad, key_rows, preferred_element_type=jnp.float32) * scale
    )
    key_grad = (
        jnp.einsum("hqk,qhd->khd", score_grad, queries, preferred_element_type=jnp.float32) * scale
    )
    return (
        query_grad.astype(jnp.bfloat16),
        key_grad.astype(jnp.bfloat16),
        value_grad.astype(jnp.bfloat16),
    )


def column_total(values):
    return jnp.sum(values.astype(jnp.float32), axis=0)


def shards(
    tokens,
    segment_ids,
    w_query,
    w_key,
    w_value,
    w_output,
    bias_query,
    bias_value,
    bias_output,
    gain_attn,
    beta_attn,
    w_inner,
    bias_inner,
    w_outer,
    bias_outer,
    gain_ffn,
    beta_ffn,
    cotangent,
):
    row_count = segment_ids.shape[0]
    slots = segment_ids.shape[1]
    model_width = tokens.shape[1]
    shaped = (row_count, slots, HEADS, model_width // HEADS)
    full_query, full_key, full_value, full_output = (
        lax.all_gather(w_query, ("dp", "tp"), axis=0, tiled=True),
        lax.all_gather(w_key, ("dp", "tp"), axis=0, tiled=True),
        lax.all_gather(w_value, ("dp", "tp"), axis=0, tiled=True),
        lax.all_gather(w_output, ("dp", "tp"), axis=0, tiled=True),
    )
    queries = (product(tokens, full_query) + bias_query).astype(jnp.bfloat16).reshape(shaped)
    key_rows = product(tokens, full_key).astype(jnp.bfloat16).reshape(shaped)
    value_rows = (product(tokens, full_value) + bias_value).astype(jnp.bfloat16).reshape(shaped)
    mixed, log_total = lax.map(attend, (queries, key_rows, value_rows, segment_ids))
    mixed = mixed.reshape(row_count * slots, model_width)
    first_sum = tokens.astype(jnp.float32) + product(mixed, full_output) + bias_output
    hidden = layer_norm(first_sum, gain_attn, beta_attn)
    hidden_low = hidden.astype(jnp.bfloat16)
    gathered = lax.all_gather(hidden_low, "tp", axis=0, tiled=True)
    inner = product(gathered, w_inner) + bias_inner
    partial_terms = product(exact_gelu(inner).astype(jnp.bfloat16), w_outer)
    outer = (
        lax.psum_scatter(
            partial_terms.astype(jnp.bfloat16), "tp", scatter_dimension=0, tiled=True
        ).astype(jnp.float32)
        + bias_outer
    )
    second_sum = hidden + outer
    layer_out = layer_norm(second_sum, gain_ffn, beta_ffn)
    out_cot = cotangent.astype(jnp.float32)
    unused_second, pull_second = jax.vjp(
        lambda resid, beta: layer_norm(resid, gain_ffn, beta), second_sum, beta_ffn
    )
    second_grad, beta_ffn_grad = pull_second(out_cot)
    outer_grad = second_grad.astype(jnp.bfloat16)
    bias_outer_grad = column_total(outer_grad)
    unused_gelu, pull_gelu = jax.vjp(exact_gelu, inner)
    grad_rows = lax.all_gather(outer_grad, "tp", axis=0, tiled=True)
    gelu_grad = product(grad_rows, w_outer.T)
    inner_grad = pull_gelu(gelu_grad)[0].astype(jnp.bfloat16)
    hidden_branch = lax.psum_scatter(
        product(inner_grad, w_inner.T).astype(jnp.bfloat16), "tp", scatter_dimension=0, tiled=True
    ).astype(jnp.float32)
    bias_inner_grad = column_total(inner_grad)
    hidden_grad = second_grad + hidden_branch
    unused_first, pull_first = jax.vjp(
        lambda resid, beta: layer_norm(resid, gain_attn, beta), first_sum, beta_attn
    )
    first_grad, beta_attn_grad = pull_first(hidden_grad)
    branch_grad = first_grad.astype(jnp.bfloat16)
    bias_output_grad = column_total(branch_grad)
    full_query, full_key, full_value, full_output = (
        lax.all_gather(w_query, ("dp", "tp"), axis=0, tiled=True),
        lax.all_gather(w_key, ("dp", "tp"), axis=0, tiled=True),
        lax.all_gather(w_value, ("dp", "tp"), axis=0, tiled=True),
        lax.all_gather(w_output, ("dp", "tp"), axis=0, tiled=True),
    )
    mixed_grad = product(branch_grad, full_output.T).astype(jnp.bfloat16).reshape(shaped)
    query_grad, key_grad, value_grad = lax.map(
        attend_back, (queries, key_rows, value_rows, segment_ids, mixed_grad, log_total)
    )
    query_grad = query_grad.reshape(row_count * slots, model_width)
    key_grad = key_grad.reshape(row_count * slots, model_width)
    value_grad = value_grad.reshape(row_count * slots, model_width)
    bias_query_grad = column_total(query_grad)
    bias_value_grad = column_total(value_grad)
    tokens_grad = (
        first_grad
        + product(query_grad, full_query.T)
        + product(key_grad, full_key.T)
        + product(value_grad, full_value.T)
    )
    totals = lax.psum(
        (
            bias_query_grad,
            bias_value_grad,
            bias_output_grad,
            beta_attn_grad,
            bias_outer_grad,
            beta_ffn_grad,
        ),
        ("dp", "tp"),
    )
    inner_total = lax.psum(bias_inner_grad, "dp")
    outer_total = totals[4]
    ffn_beta_total = totals[5]
    return (
        layer_out.astype(jnp.bfloat16),
        tokens_grad,
        totals[0],
        totals[1],
        totals[2],
        totals[3],
        inner_total,
        outer_total,
        ffn_beta_total,
    )


def solution(mesh):
    in_specs = (
        P(("dp", "tp"), None),
        P(("dp", "tp"), None),
        P(("dp", "tp"), None),
        P(("dp", "tp"), None),
        P(("dp", "tp"), None),
        P(("dp", "tp"), None),
        P(),
        P(),
        P(),
        P(),
        P(),
        P(None, "tp"),
        P("tp"),
        P("tp", None),
        P(),
        P(),
        P(),
        P(("dp", "tp"), None),
    )
    out_specs = (
        P(("dp", "tp"), None),
        P(("dp", "tp"), None),
        P(),
        P(),
        P(),
        P(),
        P("tp"),
        P(),
        P(),
    )
    return jax.shard_map(shards, mesh=mesh, in_specs=in_specs, out_specs=out_specs, check_vma=False)
```

profile of v0, /device:TPU:0, one launch (start us, length us, event | category | flops | bytes accessed | tf_op | source)
XLA Modules:
  0.0 1189.9 jit_solution(7109235398571447322)
XLA Ops:
  14.0 56.2 %all-gather.7.cloned.1.call-done = bf16[1024,1024]{1,0:T(8,128)(2,1)} async-done(((bf16[32,1024]{1,0:T(8,128)(2,1)}), bf16[1024,1024]{1,0:T(8,128)(2,1)}) %all-gather.7.cloned.1.call-update) | async-done | bytes 2097168 | tf_op jit(solution)/shard_map/all_gather | solution.py:97
  87.9 40.6 %all-gather.9.cloned.1.call-done = bf16[1024,1024]{1,0:T(8,128)(2,1)} async-done(((bf16[32,1024]{1,0:T(8,128)(2,1)}), bf16[1024,1024]{1,0:T(8,128)(2,1)}) %all-gather.9.cloned.1.call-update) | async-done | bytes 2097168 | tf_op jit(solution)/shard_map/all_gather | solution.py:95
  146.2 40.6 %all-gather.11.cloned.1.call-done = bf16[1024,1024]{1,0:T(8,128)(2,1)} async-done(((bf16[32,1024]{1,0:T(8,128)(2,1)}), bf16[1024,1024]{1,0:T(8,128)(2,1)}) %all-gather.11.cloned.1.call-update) | async-done | bytes 2097168 | tf_op jit(solution)/shard_map/all_gather | solution.py:96
  206.0 61.9 %while.26 = (s32[]{:T(128)}, bf16[2,512,16,64]{1,3,2,0:T(8,128)(2,1)}, f32[2,16,512]{2,1,0:T(8,128)S(1)}, bf16[2,512,16,64]{1,3,2,0:T(8,128)(2,1)}, s32[2,512]{1...) while((s32[]{:T(128)}, ...), condition=%wide.region_3.4_spmd, body=%wide.region_0.3_spmd.sunk | while | flops 1120731136 | bytes 55976028 | solution.py:103
  206.4 9.9 fusion.120
  225.6 11.5 fusion.122
  237.3 9.9 fusion.120
  256.5 11.2 fusion.122
  283.2 148.4 %all-gather.15.cloned.1.call-done = bf16[4096,1024]{0,1:T(8,128)(2,1)} async-done(((bf16[1024,1024]{0,1:T(8,128)(2,1)}), bf16[4096,1024]{0,1:T(8,128)(2,1)}) %all-gather.15.cloned.1.call-update) | async-done | bytes 8388624 | tf_op jit(solution)/shard_map/all_gather | solution.py:108
  431.6 46.9 %fusion.55 = (f32[4096,1024]{1,0:T(8,128)}, f32[4096,1024]{1,0:T(8,128)}) fusion(f32[1024]{0:T(1024)S(1)} %copy-done.46, bf16[4096,1024]{0,1:T(8,128)(2,1)} %all-gather.15.cloned.1.call-done, bf16[1024,1024]{1,0:T(8,128)(2,1)S(1)} %copy-done), kind=kOutput, calls=%fused_computation.66 | convolution fusion | flops 8854175744 | bytes 44044288 | tf_op jit(solution)/shard_map/dot_general | solution.py:13
  478.5 19.1 %fusion.64 = bf16[4096,1024]{0,1:T(8,128)(2,1)} fusion(bf16[1024,1024]{1,0:T(8,128)(2,1)S(1)} %copy-done.38, f32[4096,1024]{1,0:T(8,128)} %get-tuple-element.222, f32[4096,1024]{1,0:T(8,128)} %get-tuple-element.223, f32[1024]{0:T(1024)S(1)} %copy-done.46), kind=kOutput, calls=%fused_computation.86 | convolution fusion | flops 8610906112 | bytes 44044288 | tf_op jit(solution)/shard_map/dot_general | solution.py:13
  501.8 138.6 %reduce-scatter.3.cloned.1.call-done = bf16[1024,1024]{0,1:T(8,128)(2,1)} async-done(((bf16[4096,1024]{0,1:T(8,128)(2,1)}), bf16[1024,1024]{0,1:T(8,128)(2,1)}) %reduce-scatter.3.cloned.1.call-update) | async-done | bytes 2097168 | tf_op jit(solution)/shard_map/reduce_scatter | solution.py:112
  653.6 150.5 %all-gather.17.cloned.1.call-done = bf16[4096,1024]{0,1:T(8,128)(2,1)} async-done(((bf16[1024,1024]{0,1:T(8,128)(2,1)}), bf16[4096,1024]{0,1:T(8,128)(2,1)}) %all-gather.17.cloned.1.call-update) | async-done | bytes 8388624 | tf_op jit(solution)/shard_map/all_gather | solution.py:127
  804.1 24.2 %convert_reduce_fusion = (f32[1024]{0:T(1024)S(1)}, bf16[4096,1024]{1,0:T(8,128)(2,1)}) fusion(f32[4096,1024]{1,0:T(8,128)} %get-tuple-element.222, f32[4096,1024]{1,0:T(8,128)} %get-tuple-element.223, f32[1024]{0:T(1024)S(1)} %copy-done.46, bf16[4096,1024]{0,1:T(8,128)(2,1)} %all-gather.17.cloned.1.call-done, bf16[1024,1024]{1,0:T(8,128)(2,1)} %param.35), kind=kOutput, calls=%fused_computation.67 | convolution fusion | flops 8661236736 | bytes 52436992 | tf_op jit(solution)/shard_map/dot_general | solution.py:13
  828.2 14.3 %convolution_convert_fusion = bf16[4096,1024]{0,1:T(8,128)(2,1)} fusion(bf16[4096,1024]{1,0:T(8,128)(2,1)} %get-tuple-element.204, bf16[1024,1024]{1,0:T(8,128)(2,1)S(1)} %copy-done), kind=kOutput, calls=%fused_computation.87 | convolution fusion | flops 8594128896 | bytes 18874368 | tf_op jit(solution)/shard_map/dot_general | solution.py:13
  846.7 15.4 %psum.53 = f32[1024]{0:T(1024)} all-reduce(f32[1024]{0:T(1024)S(1)} %get-tuple-element.203), channel_id=1, replica_groups=mesh['dp'=8,'tp'=4] {'dp'}, use_global_device_ids=true, to_apply=%region_26.27 | all-reduce | flops 1024 | bytes 8192 | tf_op jit(solution)/shard_map/psum | solution.py:173
  862.1 123.3 %reduce-scatter.5.cloned.1.call-done = bf16[1024,1024]{0,1:T(8,128)(2,1)} async-done(((bf16[4096,1024]{0,1:T(8,128)(2,1)}), bf16[1024,1024]{0,1:T(8,128)(2,1)}) %reduce-scatter.5.cloned.1.call-update) | async-done | bytes 2097168 | tf_op jit(solution)/shard_map/reduce_scatter | solution.py:130
  1014.2 94.1 %while.27 = (s32[]{:T(128)}, bf16[2,512,16,64]{1,3,2,0:T(8,128)(2,1)}, bf16[2,512,16,64]{1,3,2,0:T(8,128)(2,1)}, bf16[2,512,16,64]{1,3,2,0:T(8,128)(2,1)}, bf16[...) while((s32[]{:T(128)}, ...), condition=%wide.region_16.17_spmd, body=%wide.region_14.16_spmd.sunk | while | flops 2724978688 | bytes 195734864 | solution.py:148
  1024.1 10.5 multiply_reduce_fusion.5
  1034.5 11.9 multiply_convert_fusion.8
  1070.8 10.5 multiply_reduce_fusion.5
  1081.3 11.9 multiply_convert_fusion.8
  1098.6 9.5 fusion.134
  1141.1 41.7 %all-reduce = (f32[1024]{0:T(1024)}, f32[1024]{0:T(1024)}, f32[1024]{0:T(1024)}, f32[1024]{0:T(1024)}, f32[1024]{0:T(1024)}, /*index=5*/f32[1024]{0:T(1024)}) all-reduce(f32[1024]{0:T(1024)S(1)} %reduce_sum.171, f32[1024]{0:T(1024)S(1)} %reduce_sum.177, f32[1024]{0:T(1024)S(1)} %copy-done.35, ...), channel_id=1, replica_groups=mesh['dp'=8,'tp'=4] {'dp','tp'}, use_global_device_ids=true, to_apply=%region_18.19 | all-reduce | flops 6144 | bytes 49152 | tf_op jit(solution)/shard_map/psum | solution.py:162
  (202 shorter events, 217.4 us)
Async XLA Ops:
  7.2 424.5 %copy-start = (bf16[1024,1024]{1,0:T(8,128)(2,1)S(1)}, bf16[1024,1024]{1,0:T(8,128)(2,1)}, u32[]{:S(2)}) copy-start(bf16[1024,1024]{1,0:T(8,128)(2,1)} %param.33) | copy-start | bytes 6291460
  7.2 63.0 %copy-start.43 = (f32[1024]{0:T(1024)S(1)}, f32[1024]{0:T(1024)}, u32[]{:S(2)}) copy-start(f32[1024]{0:T(1024)} %param.29) | copy-start | bytes 12292
  7.2 63.0 %all-gather.7.cloned.1.call-start = ((), (), s32[]{:S(2)}) async-start(), calls=%async_computation.2 | async-start | bytes 2162688 | tf_op jit(solution)/shard_map/all_gather | solution.py:97
  7.9 120.5 %all-gather.9.cloned.1.call-start = ((), (), s32[]{:S(2)}) async-start(), calls=%async_computation.3 | async-start | bytes 2162688 | tf_op jit(solution)/shard_map/all_gather | solution.py:95
  8.7 178.1 %all-gather.11.cloned.1.call-start = ((), (), s32[]{:S(2)}) async-start(), calls=%async_computation.4 | async-start | bytes 2162688 | tf_op jit(solution)/shard_map/all_gather | solution.py:96
  9.4 264.2 %all-gather.13.cloned.1.call-start = ((), (), s32[]{:S(2)}) async-start(), calls=%async_computation.5 | async-start | bytes 2162688 | tf_op jit(solution)/shard_map/all_gather | solution.py:98
  10.0 421.6 %all-gather.15.cloned.1.call-start = ((), (), s32[]{:S(2)}) async-start(), calls=%async_computation.6 | async-start | bytes 10485760 | tf_op jit(solution)/shard_map/all_gather | solution.py:108
  82.4 46.1 %copy-start.44 = (f32[1024]{0:T(1024)S(1)}, f32[1024]{0:T(1024)}, u32[]{:S(2)}) copy-start(f32[1024]{0:T(1024)} %param.28) | copy-start | bytes 12292
  281.1 150.5 %copy-start.46 = (f32[1024]{0:T(1024)S(1)}, f32[1024]{0:T(1024)}, u32[]{:S(2)}) copy-start(f32[1024]{0:T(1024)} %param.34) | copy-start | bytes 12292
  283.2 357.3 %reduce-scatter.3.cloned.1.call-start = ((), (), s32[]{:S(2)}) async-start(), calls=%async_computation.7 | async-start | bytes 10485760 | tf_op jit(solution)/shard_map/reduce_scatter | solution.py:112
  431.6 46.9 %copy-start.38 = (bf16[1024,1024]{1,0:T(8,128)(2,1)S(1)}, bf16[1024,1024]{1,0:T(8,128)(2,1)}, u32[]{:S(2)}) copy-start(bf16[1024,1024]{1,0:T(8,128)(2,1)} %param.35) | copy-start | bytes 6291460
  497.7 142.8 %copy-start.36 = (f32[1024]{0:T(1024)S(1)}, f32[1024]{0:T(1024)}, u32[]{:S(2)}) copy-start(f32[1024]{0:T(1024)} %param.36) | copy-start | bytes 12292
  497.7 306.4 %all-gather.17.cloned.1.call-start = ((), (), s32[]{:S(2)}) async-start(), calls=%async_computation.8 | async-start | bytes 10485760 | tf_op jit(solution)/shard_map/all_gather | solution.py:127
  501.8 142.3 %copy-start.31 = (f32[1024]{0:T(1024)S(1)}, f32[1024]{0:T(1024)}, u32[]{:S(2)}) copy-start(f32[1024]{0:T(1024)} %param.37) | copy-start | bytes 12292
  653.5 331.9 %reduce-scatter.5.cloned.1.call-start = ((), (), s32[]{:S(2)}) async-start(), calls=%async_computation.9 | async-start | bytes 10485760 | tf_op jit(solution)/shard_map/reduce_scatter | solution.py:130
  862.1 129.4 %copy-start.27 = (f32[1024]{0:T(1024)S(1)}, f32[1024]{0:T(1024)}, u32[]{:S(2)}) copy-start(f32[1024]{0:T(1024)} %copy-done.26) | copy-start | bytes 12292
  1014.8 9.2 copy-start.5
  1014.9 9.2 copy-start.9
  1034.5 11.9 copy-start.6
  1034.5 11.9 copy-start.17
  1061.6 9.2 copy-start.5
  1081.3 11.9 copy-start.6
  1081.3 11.9 copy-start.17
  1131.0 51.8 %copy-start.1 = (bf16[1024,1024]{1,0:T(8,128)(2,1)S(1)}, bf16[1024,1024]{1,0:T(8,128)(2,1)}, u32[]{:S(2)}) copy-start(bf16[1024,1024]{1,0:T(8,128)(2,1)} %param.33) | copy-start | bytes 6291460
  (38 other events, 137.4 us)
Sparse Core Ops, SparseCore 0:
  11.0 59.1 all-gather.6
  73.1 55.3 all-gather.8
  131.4 55.3 all-gather.10
  189.6 55.3 all-gather.12
  283.3 148.3 all-gather.14
  497.8 142.6 reduce-scatter.2
  653.7 150.3 all-gather.16
  842.7 142.6 reduce-scatter.4
where the time goes:
time: 1200 us; the launch traced here: 1190 us
  waiting for transfers between devices  701 us (58%)
  matrix products  249 us (21%)
  local copies, waits for them, and re-layouts  99.4 us (8%)
  other arithmetic  67.7 us (6%)
  blocking collectives  57 us (5%)
  between operations  14.8 us (1%)
    all_gather x1, waiting for transfers between devices, shards(): grad_rows = lax.all_gather(outer_grad, 'tp', axis=0, tiled=True)  150 us
    all_gather x1, waiting for transfers between devices, shards(): gathered = lax.all_gather(hidden_low, 'tp', axis=0, tiled=True)  148 us
    dot_general x12, matrix products, product(): return jnp.dot(left, right, preferred_element_type=jnp.float32)  140 us
    reduce_scatter x1, waiting for transfers between devices, shards(): lax.psum_scatter(partial_terms.astype(jnp.bfloat16), 'tp', scatter_dimens...  139 us
    reduce_scatter x1, waiting for transfers between devices, shards(): lax.psum_scatter(product(inner_grad, w_inner.T).astype(jnp.bfloat16), 'tp...  123 us
    all_gather x1, waiting for transfers between devices, shards(): lax.all_gather(w_value, ('dp', 'tp'), axis=0, tiled=True)  56.2 us
    psum x1, blocking collectives, shards(): lax.psum((bias_query_grad, bias_value_grad, bias_output_grad, beta_attn_g...  41.7 us
    all_gather x1, waiting for transfers between devices, shards(): lax.all_gather(w_key, ('dp', 'tp'), axis=0, tiled=True)  40.6 us
  transfers between devices with their start and end apart: 8, of which 7 were waited for; matrix products, arithmetic and copies ran while one was open for 11% of the time, Pallas kernels for 0%

commit v1 on v0

v1 whole, which is shorter than its diff:
```python
import functools
import math

import jax
import jax.numpy as jnp
from jax import lax
from jax.experimental import pallas as pl
from jax.experimental.pallas import tpu as pltpu
from jax.sharding import Mesh
from jax.sharding import PartitionSpec as P

HEADS = 16
F32 = jnp.float32
BF16 = jnp.bfloat16
NORM_EPSILON = 1e-12
LOG2E = math.log2(math.e)
LN2 = math.log(2.0)
VMEM_LIMIT = 56 * 1024 * 1024


def dot(left, right):
    return jnp.dot(left, right, preferred_element_type=F32)


def dot_nt(left, right):
    return lax.dot_general(left, right, (((1,), (1,)), ((), ())), preferred_element_type=F32)


def column_sum(values):
    return jnp.sum(values.astype(F32), axis=0, keepdims=True)


def normalize(resid):
    centered = resid - jnp.mean(resid, axis=-1, keepdims=True)
    spread = jnp.mean(centered * centered, axis=-1, keepdims=True)
    scale = lax.rsqrt(spread + NORM_EPSILON)
    return centered * scale, scale


def norm_back(grad, gain, normal, scale):
    weighted = grad * gain
    return scale * (
        weighted
        - jnp.mean(weighted, axis=-1, keepdims=True)
        - normal * jnp.mean(weighted * normal, axis=-1, keepdims=True)
    )


def gelu_parts(value):
    size = jnp.abs(value)
    step = 1.0 / (1.0 + (0.3275911 / math.sqrt(2.0)) * size)
    bell = jnp.exp2(value * value * (-0.5 * LOG2E))
    series = step * (
        0.5 * 0.254829592
        + step
        * (
            0.5 * -0.284496736
            + step * (0.5 * 1.421413741 + step * (0.5 * -1.453152027 + step * (0.5 * 1.061405429)))
        )
    )
    tail = series * bell
    share = jnp.where(value >= 0, 1.0 - tail, tail)
    return value * share, share + value * bell * (1.0 / math.sqrt(2.0 * math.pi))


def attend_kernel(
    head_size, seg_row, seg_col, x, wq, wk, wv, bq, bv, q_out, k_out, v_out, probs_out, mixed_out
):
    rows, slots = seg_row.shape[0], seg_row.shape[2]
    group = wq.shape[1] // head_size
    factor = head_size ** (-0.5) * LOG2E
    q_out[...] = ((dot(x[...], wq[...]) + bq[...]) * factor).astype(BF16)
    k_out[...] = dot(x[...], wk[...]).astype(BF16)
    v_out[...] = (dot(x[...], wv[...]) + bv[...]).astype(BF16)
    for row in range(rows):
        span = slice(row * slots, (row + 1) * slots)
        same_doc = seg_col[span, :] == seg_row[row]
        pieces = []
        for head in range(group):
            lanes = slice(head * head_size, (head + 1) * head_size)
            scores = dot_nt(k_out[span, lanes], q_out[span, lanes])
            scores = jnp.where(same_doc, scores, -1000000000.0)
            top = jnp.max(scores, axis=0, keepdims=True)
            powers = jnp.exp2(scores - top)
            total = jnp.sum(powers, axis=0, keepdims=True)
            probs = (powers * (1.0 / total)).astype(BF16)
            probs_out[0, row * group + head] = probs
            pieces.append(dot(v_out[span, lanes].T, probs))
        mixed_out[span, :] = jnp.concatenate(pieces, axis=0).T.astype(BF16)


def attend(tokens, segments, wq, wk, wv, bq, bv):
    count, width = tokens.shape
    rows, slots = segments.shape
    head_size = width // HEADS
    groups = 4
    lanes = width // groups
    heads = HEADS // groups
    whole = lambda shape: pl.BlockSpec(shape, lambda g: (0,) * len(shape))
    column = lambda height: pl.BlockSpec((height, lanes), lambda g: (0, g))
    return pl.pallas_call(
        functools.partial(attend_kernel, head_size),
        grid=(groups,),
        in_specs=[
            whole((rows, 1, slots)),
            whole((count, 1)),
            whole((count, width)),
            column(width),
            column(width),
            column(width),
            column(1),
            column(1),
        ],
        out_specs=[
            column(count),
            column(count),
            column(count),
            pl.BlockSpec((1, rows * heads, slots, slots), lambda g: (g, 0, 0, 0)),
            column(count),
        ],
        out_shape=[
            jax.ShapeDtypeStruct((count, width), BF16),
            jax.ShapeDtypeStruct((count, width), BF16),
            jax.ShapeDtypeStruct((count, width), BF16),
            jax.ShapeDtypeStruct((groups, rows * heads, slots, slots), BF16),
            jax.ShapeDtypeStruct((count, width), BF16),
        ],
        compiler_params=pltpu.CompilerParams(vmem_limit_bytes=VMEM_LIMIT),
        cost_estimate=pl.CostEstimate(
            flops=6 * count * width * width + 16 * count * slots * width,
            bytes_accessed=40 * 2**20,
            transcendentals=count * slots * HEADS,
        ),
        name="attend",
    )(segments.reshape(rows, 1, slots), segments.reshape(count, 1), tokens, wq, wk, wv, bq, bv)


def first_norm_kernel(x, mixed, wo, bo, normal_out, scale_out):
    resid = x[...].astype(F32) + dot(mixed[...], wo[...]) + bo[...]
    normal_out[...], scale_out[...] = normalize(resid)


def first_norm(tokens, mixed, wo, bo):
    count, width = tokens.shape
    tile = 256
    whole = lambda shape: pl.BlockSpec(shape, lambda i: (0,) * len(shape))
    rows = lambda cols: pl.BlockSpec((tile, cols), lambda i: (i, 0))
    return pl.pallas_call(
        first_norm_kernel,
        grid=(count // tile,),
        in_specs=[rows(width), rows(width), whole((width, width)), whole((1, width))],
        out_specs=[rows(width), rows(1)],
        out_shape=[
            jax.ShapeDtypeStruct((count, width), F32),
            jax.ShapeDtypeStruct((count, 1), F32),
        ],
        compiler_params=pltpu.CompilerParams(vmem_limit_bytes=VMEM_LIMIT),
        cost_estimate=pl.CostEstimate(
            flops=2 * count * width * width, bytes_accessed=10 * 2**20, transcendentals=0
        ),
        name="first_norm",
    )(tokens, mixed, wo, bo)


TILE = 256


def inner_kernel(normal, gain, beta, w_in, b_in, w_out, outer, slope_out, hidden):
    part = pl.program_id(0)

    @pl.when(part == 0)
    def _():
        hidden[...] = (normal[...] * gain[...] + beta[...]).astype(BF16)
        outer[...] = jnp.zeros_like(outer)

    for start in range(0, hidden.shape[0], TILE):
        span = slice(start, start + TILE)
        act, slope = gelu_parts(dot(hidden[span, :], w_in[...]) + b_in[...])
        slope_out[span, :] = slope.astype(BF16)
        outer[span, :] += dot(act.astype(BF16), w_out[...])


def inner_forward(normal, gain, beta, w_in, b_in, w_out):
    count, width = normal.shape
    units = w_in.shape[1]
    block = 1024
    whole = lambda shape: pl.BlockSpec(shape, lambda i: (0,) * len(shape))
    return pl.pallas_call(
        inner_kernel,
        grid=(units // block,),
        in_specs=[
            whole((count, width)),
            whole((1, width)),
            whole((1, width)),
            pl.BlockSpec((width, block), lambda i: (0, i)),
            pl.BlockSpec((1, block), lambda i: (0, i)),
            pl.BlockSpec((block, width), lambda i: (i, 0)),
        ],
        out_specs=[whole((count, width)), pl.BlockSpec((count, block), lambda i: (0, i))],
        out_shape=[
            jax.ShapeDtypeStruct((count, width), F32),
            jax.ShapeDtypeStruct((count, units), BF16),
        ],
        scratch_shapes=[pltpu.VMEM((count, width), BF16)],
        compiler_params=pltpu.CompilerParams(vmem_limit_bytes=VMEM_LIMIT),
        cost_estimate=pl.CostEstimate(
            flops=4 * count * width * units, bytes_accessed=32 * 2**20, transcendentals=0
        ),
        name="inner_forward",
    )(normal, gain, beta, w_in, b_in, w_out)


def inner_back_kernel(
    normal,
    scale,
    gain_attn,
    beta_attn,
    outer,
    b_out,
    gain_ffn,
    beta_ffn,
    cot,
    slope,
    w_in,
    w_out,
    layer_out,
    first_grad,
    branch_grad,
    sum_inner,
    sum_outer,
    sum_beta_ffn,
    sum_beta_attn,
    sum_output,
    hidden_grad,
    outer_grad,
):
    part = pl.program_id(0)
    count = normal.shape[0]

    @pl.when(part == 0)
    def _():
        sum_outer[...] = jnp.zeros_like(sum_outer)
        sum_beta_ffn[...] = jnp.zeros_like(sum_beta_ffn)
        for start in range(0, count, TILE):
            span = slice(start, start + TILE)
            hidden = normal[span, :] * gain_attn[...] + beta_attn[...]
            unit, scale_two = normalize(hidden + outer[span, :] + b_out[...])
            layer_out[span, :] = (unit * gain_ffn[...] + beta_ffn[...]).astype(BF16)
            grad = cot[span, :].astype(F32)
            sum_beta_ffn[...] += column_sum(grad)
            second = norm_back(grad, gain_ffn[...], unit, scale_two)
            hidden_grad[span, :] = second
            low = second.astype(BF16)
            outer_grad[span, :] = low
            sum_outer[...] += column_sum(low)

    total = jnp.zeros(sum_inner.shape, F32)
    for start in range(0, count, TILE):
        span = slice(start, start + TILE)
        back = dot_nt(outer_grad[span, :], w_out[...])
        inner_grad = (slope[span, :].astype(F32) * back).astype(BF16)
        total += column_sum(inner_grad)
        hidden_grad[span, :] += dot_nt(inner_grad, w_in[...])
    sum_inner[...] = total

    @pl.when(part == pl.num_programs(0) - 1)
    def _():
        sum_beta_attn[...] = jnp.zeros_like(sum_beta_attn)
        sum_output[...] = jnp.zeros_like(sum_output)
        for start in range(0, count, TILE):
            span = slice(start, start + TILE)
            grad = hidden_grad[span, :]
            sum_beta_attn[...] += column_sum(grad)
            first = norm_back(grad, gain_attn[...], normal[span, :], scale[span, :])
            first_grad[span, :] = first
            low = first.astype(BF16)
            branch_grad[span, :] = low
            sum_output[...] += column_sum(low)


def inner_backward(
    normal, scale, gain_attn, beta_attn, outer, b_out, gain_ffn, beta_ffn, cot, slope, w_in, w_out
):
    count, width = normal.shape
    units = w_in.shape[1]
    block = 1024
    once = dict(pipeline_mode=pl.Buffered(1))
    whole = lambda shape: pl.BlockSpec(shape, lambda i: (0,) * len(shape), **once)
    vector = whole((1, width))
    shaped = jax.ShapeDtypeStruct
    return pl.pallas_call(
        inner_back_kernel,
        grid=(units // block,),
        in_specs=[
            whole((count, width)),
            whole((count, 1)),
            vector,
            vector,
            whole((count, width)),
            vector,
            vector,
            vector,
            whole((count, width)),
            pl.BlockSpec((count, block), lambda i: (0, i)),
            pl.BlockSpec((width, block), lambda i: (0, i)),
            pl.BlockSpec((block, width), lambda i: (i, 0)),
        ],
        out_specs=[
            whole((count, width)),
            whole((count, width)),
            whole((count, width)),
            pl.BlockSpec((1, block), lambda i: (0, i)),
            vector,
            vector,
            vector,
            vector,
        ],
        out_shape=[
            shaped((count, width), BF16),
            shaped((count, width), F32),
            shaped((count, width), BF16),
            shaped((1, units), F32),
            shaped((1, width), F32),
            shaped((1, width), F32),
            shaped((1, width), F32),
            shaped((1, width), F32),
        ],
        scratch_shapes=[pltpu.VMEM((count, width), F32), pltpu.VMEM((count, width), BF16)],
        compiler_params=pltpu.CompilerParams(vmem_limit_bytes=VMEM_LIMIT),
        cost_estimate=pl.CostEstimate(
            flops=4 * count * width * units, bytes_accessed=46 * 2**20, transcendentals=0
        ),
        name="inner_backward",
    )(normal, scale, gain_attn, beta_attn, outer, b_out, gain_ffn, beta_ffn, cot, slope, w_in, w_out)


def attend_back_kernel(
    head_size, slots, branch, wo, q, k, v, mixed, probs_in, dq_out, dk_out, dv_out, sum_q, sum_v
):
    rows = branch.shape[0] // slots
    group = wo.shape[0] // head_size
    mixed_grad = dot_nt(branch[...], wo[...])
    low_grad = mixed_grad.astype(BF16)
    product = low_grad.astype(F32) * mixed[...].astype(F32)
    for row in range(rows):
        span = slice(row * slots, (row + 1) * slots)
        turned = product[span, :].T
        keys_turned = k[span, :].T
        queries_grad = []
        keys_grad = []
        values_grad = []
        for head in range(group):
            lanes = slice(head * head_size, (head + 1) * head_size)
            probs = probs_in[0, row * group + head]
            grad = low_grad[span, lanes]
            shift = jnp.sum(turned[lanes, :], axis=0, keepdims=True)
            reach = dot_nt(v[span, lanes], grad)
            score_grad = (probs.astype(F32) * (reach - shift)).astype(BF16)
            values_grad.append(dot(probs, grad))
            keys_grad.append(dot(score_grad, q[span, lanes]))
            queries_grad.append(dot(keys_turned[lanes, :], score_grad))
        dv_out[span, :] = jnp.concatenate(values_grad, axis=1).astype(BF16)
        dk_out[span, :] = (jnp.concatenate(keys_grad, axis=1) * LN2).astype(BF16)
        dq_out[span, :] = (jnp.concatenate(queries_grad, axis=0).T * head_size ** (-0.5)).astype(BF16)
    sum_q[...] = column_sum(dq_out[...])
    sum_v[...] = column_sum(dv_out[...])


def attend_backward(branch, wo, q, k, v, mixed, probs, slots):
    count, width = branch.shape
    groups, units = probs.shape[:2]
    lanes = width // groups
    column = lambda height: pl.BlockSpec((height, lanes), lambda g: (0, g))
    shaped = jax.ShapeDtypeStruct
    return pl.pallas_call(
        functools.partial(attend_back_kernel, width // HEADS, slots),
        grid=(groups,),
        in_specs=[
            pl.BlockSpec((count, width), lambda g: (0, 0)),
            pl.BlockSpec((lanes, width), lambda g: (g, 0)),
            column(count),
            column(count),
            column(count),
            column(count),
            pl.BlockSpec((1, units, slots, slots), lambda g: (g, 0, 0, 0)),
        ],
        out_specs=[column(count), column(count), column(count), column(1), column(1)],
        out_shape=[
            shaped((count, width), BF16),
            shaped((count, width), BF16),
            shaped((count, width), BF16),
            shaped((1, width), F32),
            shaped((1, width), F32),
        ],
        compiler_params=pltpu.CompilerParams(vmem_limit_bytes=VMEM_LIMIT),
        cost_estimate=pl.CostEstimate(
            flops=2 * count * width * width + 32 * count * slots * width,
            bytes_accessed=36 * 2**20,
            transcendentals=0,
        ),
        name="attend_backward",
    )(branch, wo, q, k, v, mixed, probs)


def tokens_grad_kernel(first, dq, dk, dv, wq, wk, wv, out):
    out[...] = (
        first[...] + dot_nt(dq[...], wq[...]) + dot_nt(dk[...], wk[...]) + dot_nt(dv[...], wv[...])
    )


def tokens_backward(first, dq, dk, dv, wq, wk, wv):
    count, width = first.shape
    tile = 256
    rows = pl.BlockSpec((tile, width), lambda i: (i, 0))
    whole = pl.BlockSpec((width, width), lambda i: (0, 0))
    return pl.pallas_call(
        tokens_grad_kernel,
        grid=(count // tile,),
        in_specs=[rows, rows, rows, rows, whole, whole, whole],
        out_specs=rows,
        out_shape=jax.ShapeDtypeStruct((count, width), F32),
        compiler_params=pltpu.CompilerParams(vmem_limit_bytes=VMEM_LIMIT),
        cost_estimate=pl.CostEstimate(
            flops=6 * count * width * width, bytes_accessed=20 * 2**20, transcendentals=0
        ),
        name="tokens_backward",
    )(first, dq, dk, dv, wq, wk, wv)


ALL = ("quad", "core", "tp")
DATA = ("quad", "core")


def gather_weights(w_query, w_key, w_value, w_output, w_inner, w_outer):
    parts = lax.axis_size(DATA)
    tp = lax.axis_size("tp")
    place = lax.axis_index(DATA)
    width = w_query.shape[1]
    attn = lax.all_gather(jnp.stack([w_query, w_key, w_value, w_output]), ALL, axis=1, tiled=True)
    step = w_inner.shape[0] // parts
    own = lax.dynamic_slice_in_dim(w_inner, place * step, step, 0)
    full_inner = lax.all_gather(own, ALL, axis=0)
    full_inner = full_inner.reshape(parts, tp, step, -1).transpose(0, 2, 1, 3).reshape(width, -1)
    step = w_outer.shape[0] // parts
    own = lax.dynamic_slice_in_dim(w_outer, place * step, step, 0)
    full_outer = lax.all_gather(own, ALL, axis=0)
    full_outer = full_outer.reshape(parts, tp, step, width).transpose(1, 0, 2, 3).reshape(-1, width)
    return attn[0], attn[1], attn[2], attn[3], full_inner, full_outer


def shards(
    tokens,
    segment_ids,
    w_query,
    w_key,
    w_value,
    w_output,
    bias_query,
    bias_value,
    bias_output,
    gain_attn,
    beta_attn,
    w_inner,
    bias_inner,
    w_outer,
    bias_outer,
    gain_ffn,
    beta_ffn,
    cotangent,
):
    slots = segment_ids.shape[1]
    line = lambda vector: vector.reshape(1, -1)
    full_query, full_key, full_value, full_output, full_inner, full_outer = gather_weights(
        w_query, w_key, w_value, w_output, w_inner, w_outer
    )
    bias_inner = lax.all_gather(bias_inner, "tp", axis=0, tiled=True)
    q, k, v, probs, mixed = attend(
        tokens, segment_ids, full_query, full_key, full_value, line(bias_query), line(bias_value)
    )
    normal, scale = first_norm(tokens, mixed, full_output, line(bias_output))
    outer, slope = inner_forward(
        normal, line(gain_attn), line(beta_attn), full_inner, line(bias_inner), full_outer
    )
    layer_out, first_grad, branch, sum_inner, sum_outer, sum_beta_ffn, sum_beta_attn, sum_output = (
        inner_backward(
            normal,
            scale,
            line(gain_attn),
            line(beta_attn),
            outer,
            line(bias_outer),
            line(gain_ffn),
            line(beta_ffn),
            cotangent,
            slope,
            full_inner,
            full_outer,
        )
    )
    dq, dk, dv, sum_q, sum_v = attend_backward(branch, full_output, q, k, v, mixed, probs, slots)
    tokens_grad = tokens_backward(first_grad, dq, dk, dv, full_query, full_key, full_value)
    totals = lax.psum(
        jnp.concatenate(
            [sum_q, sum_v, sum_output, sum_beta_attn, sum_outer, sum_beta_ffn, sum_inner], axis=1
        )[0],
        ALL,
    )
    width = tokens.shape[1]
    six = [totals[i * width : (i + 1) * width] for i in range(6)]
    units = w_inner.shape[1]
    inner_total = lax.dynamic_slice_in_dim(
        totals[6 * width :], lax.axis_index("tp") * units, units, 0
    )
    return (
        layer_out,
        tokens_grad,
        six[0],
        six[1],
        six[2],
        six[3],
        inner_total,
        six[4],
        six[5],
    )


def solution(mesh):
    dp, tp = mesh.shape["dp"], mesh.shape["tp"]
    split = Mesh(mesh.devices.reshape(dp // 2, 2, tp), ALL)
    spread = P(ALL, None)
    in_specs = (
        (spread,) * 6
        + (P(),) * 5
        + (P(None, "tp"), P("tp"), P("tp", None), P(), P(), P(), spread)
    )
    out_specs = (spread, spread, P(), P(), P(), P(), P("tp"), P(), P())
    return jax.shard_map(shards, mesh=split, in_specs=in_specs, out_specs=out_specs, check_vma=False)
```

time: 1200 us -> 462 us (0.39)
  waiting for transfers between devices: 701 us -> 188 us
  matrix products: 249 us -> 0 us
  Pallas kernels: 0 us -> 150 us
  other arithmetic: 67.7 us -> 1.67 us
  local copies, waits for them, and re-layouts: 99.4 us -> 46.7 us
    reduce_scatter x2 -> x0, waiting for transfers between devices: 262 us -> none  [the longest x1 139 us: shards(): lax.psum_scatter(partial_terms.astype(jnp.bfloat16), 'tp', scatter_dimens...]
    all_gather x6 -> x3, waiting for transfers between devices: 436 us -> 187 us  [the longest x1 71.5 us: gather_weights(): lax.all_gather(jnp.stack([w_query, w_key, w_value, w_output]), ALL, axis=...]
    dot_general x26 -> x0, matrix products: 249 us -> none  [the longest x12 140 us: product(): return jnp.dot(left, right, preferred_element_type=jnp.float32)]
    pallas_call x0 -> x6, Pallas kernels: none -> 150 us  [the longest x1 34.9 us: inner_backward(): pl.pallas_call(inner_back_kernel, grid=(units // block,), in_specs=[whole...]
    reduce_sum x11 -> x0, other arithmetic: 41 us -> none  [the longest x2 18.4 us: attend(): log_total = jax.nn.logsumexp(scores, axis=-1)]
    while x36 -> x0, local copies, waits for them, and re-layouts: 39.5 us -> none  [the longest x4 20.2 us: shards(): lax.map(attend, (queries, key_rows, value_rows, segment_ids))]
    convert_element_type x3 -> x0, other arithmetic: 25.7 us -> none  [the longest x2 23.7 us: attend_back(): score_grad = (probs * (prob_grad - inner_sum)).astype(jnp.bfloat16)]
    psum x2 -> x1, blocking collectives: 57 us -> 39.6 us  [shards(): lax.psum(jnp.concatenate([sum_q, sum_v, sum_output, sum_beta_attn, sum_ou...]
  transfers between devices with their start and end apart: 8 -> 3, of which waited for: 7 -> 3; matrix products, arithmetic and copies ran while one was open for 11% -> 8% of each run, Pallas kernels for 0% -> 0%
where the time goes in v1:
time: 462 us; the launch traced here: 455 us
  waiting for transfers between devices  188 us (41%)
  Pallas kernels  150 us (32%)
  blocking collectives  55 us (12%)
  local copies, waits for them, and re-layouts  46.7 us (10%)
  between operations  14.4 us (3%)
    all_gather x1, waiting for transfers between devices, gather_weights(): lax.all_gather(jnp.stack([w_query, w_key, w_value, w_output]), ALL, axis=...  71.5 us
    all_gather x1, waiting for transfers between devices, gather_weights(): full_inner = lax.all_gather(own, ALL, axis=0)  61.2 us
    all_gather x1, waiting for transfers between devices, gather_weights(): full_outer = lax.all_gather(own, ALL, axis=0)  54.8 us
    psum x1, blocking collectives, shards(): lax.psum(jnp.concatenate([sum_q, sum_v, sum_output, sum_beta_attn, sum_ou...  39.6 us
    pallas_call x1, Pallas kernels, inner_backward(): pl.pallas_call(inner_back_kernel, grid=(units // block,), in_specs=[whole...  34.9 us
    pallas_call x1, Pallas kernels, inner_forward(): pl.pallas_call(inner_kernel, grid=(units // block,), in_specs=[whole((cou...  33.4 us
    pallas_call x1, Pallas kernels, attend(): pl.pallas_call(functools.partial(attend_kernel, head_size), grid=(groups,...  31.6 us
    pallas_call x1, Pallas kernels, attend_backward(): pl.pallas_call(functools.partial(attend_back_kernel, width // HEADS, slot...  29.6 us
  transfers between devices with their start and end apart: 3, of which 3 were waited for; matrix products, arithmetic and copies ran while one was open for 8% of the time, Pallas kernels for 0%

profile of v1, /device:TPU:0, one launch (start us, length us, event | category | flops | bytes accessed | tf_op | source)
XLA Modules:
  0.0 454.9 jit_solution(14844302912680052172)
XLA Ops:
  7.3 1.5 copy-done
  8.8 0.7 constant_dynamic-slice_fusion.1
  9.6 1.7 constant_dynamic-slice_fusion
  11.3 1.7 pad_maximum_fusion
  13.1 0.6 reshape.65.seg_row
  13.7 1.0 copy.36
  14.7 15.3 %all_gather.21 = f32[4096]{0:T(1024)} all-gather(f32[1024]{0:T(1024)S(1)} %copy-done.4), channel_id=1, replica_groups=mesh['quad'=4,'core'=2,'tp'=4] {'tp'}, dimensions={0}, use_global_device_ids=true | all-gather | bytes 20480 | tf_op jit(solution)/shard_map/all_gather | solution.py:476
  30.0 61.2 %all-gather.8.cloned.1.call-done = bf16[4096,1024]{1,0:T(8,128)(2,1)} async-done(((bf16[128,1024]{1,0:T(8,128)(2,1)}), bf16[4096,1024]{1,0:T(8,128)(2,1)}) %all-gather.8.cloned.1.call-update) | async-done | bytes 8388624 | tf_op jit(solution)/shard_map/all_gather | solution.py:442
  91.2 12.1 %copy.33 = bf16[8,4,128,1024]{3,1,2,0:T(4,128)(2,1)} copy(bf16[8,4,128,1024]{3,2,1,0:T(8,128)(2,1)} %bitcast.36) | data formatting | bytes 16777216 | tf_op jit(solution)/shard_map/reshape | solution.py:443
  103.3 12.1 %copy.37 = bf16[128,8,4,1024]{3,1,2,0:T(8,128)(2,1)} copy(bf16[128,8,4,1024]{3,2,1,0:T(4,128)(2,1)} %bitcast.35) | data formatting | bytes 16777216
  115.5 54.8 %all-gather.10.cloned.1.call-done = bf16[4096,1024]{1,0:T(8,128)(2,1)} async-done(((bf16[128,1024]{1,0:T(8,128)(2,1)}), bf16[4096,1024]{1,0:T(8,128)(2,1)}) %all-gather.10.cloned.1.call-update) | async-done | bytes 8388624 | tf_op jit(solution)/shard_map/all_gather | solution.py:446
  170.3 8.2 %copy.34 = bf16[8,4,128,1024]{3,2,0,1:T(8,128)(2,1)} copy(bf16[8,4,128,1024]{3,2,1,0:T(8,128)(2,1)} %bitcast.37) | data formatting | bytes 16777216 | tf_op jit(solution)/shard_map/reshape | solution.py:447
  178.5 71.5 %all-gather.6.cloned.1.call-done = bf16[4,1024,1024]{2,1,0:T(8,128)(2,1)} async-done(((bf16[4,32,1024]{2,1,0:T(8,128)(2,1)}), bf16[4,1024,1024]{2,1,0:T(8,128)(2,1)}) %all-gather.6.cloned.1.call-update) | async-done | bytes 8388624 | tf_op jit(solution)/shard_map/all_gather | solution.py:439
  249.9 6.0 %slice_bitcast_fusion = (bf16[1024,1024]{1,0:T(8,128)(2,1)}, bf16[1024,1024]{1,0:T(8,128)(2,1)}, bf16[1024,1024]{1,0:T(8,128)(2,1)}, bf16[1024,1024]{1,0:T(8,128)(2,1)}) fusion(bf16[4,1024,1024]{2,1,0:T(8,128)(2,1)} %all-gather.6.cloned.1.call-done), kind=kLoop, calls=%fused_computation | loop fusion | bytes 16777216 | tf_op jit(solution)/shard_map/squeeze | solution.py:448
  255.9 31.6 %attend.1 = (bf16[1024,1024]{1,0:T(8,128)(2,1)}, bf16[1024,1024]{1,0:T(8,128)(2,1)}, bf16[1024,1024]{1,0:T(8,128)(2,1)}, bf16[4,8,512,512]{3,2,1,0:T(8,128)(2,1)}, bf16[1024,1024]{1,0:T(8,128)(2,1)}) custom-call(s32[2,1,512]{2,1,0:T(1,128)} %reshape.65.seg_row, s32[1024,1]{1,0:T(8,128)} %bitcast.42, bf16[1024,1024]{1,0:T(8,128)(2,1)} %x.3, ...), custom_call_target="tpu_custom_call" | custom-call | flops 15032385536 | bytes 41943040 | tf_op jit(solution)/shard_map/attend/pallas_call | solution.py:101
  287.6 7.6 %first_norm.1 = (f32[1024,1024]{1,0:T(8,128)}, f32[1024,1]{1,0:T(8,128)}) custom-call(bf16[1024,1024]{1,0:T(8,128)(2,1)} %x.3, bf16[1024,1024]{1,0:T(8,128)(2,1)} %get-tuple-element.31.mixed, bf16[1024,1024]{1,0:T(8,128)(2,1)} %get-tuple-element.53.wo, f32[1,1024]{1,0:T(1,128)} %bitcast.53), custom_call_target="tpu_custom_call" | custom-call | flops 2147483648 | bytes 10485760 | tf_op jit(solution)/shard_map/first_norm/pallas_call | solution.py:148
  295.1 33.4 %inner_forward.1 = (f32[1024,1024]{1,0:T(8,128)}, bf16[1024,4096]{1,0:T(8,128)(2,1)}) custom-call(f32[1024,1024]{1,0:T(8,128)} %get-tuple-element.32.normal, f32[1,1024]{1,0:T(1,128)} %bitcast.54, f32[1,1024]{1,0:T(1,128)} %bitcast.56, bf16[1024,4096]{1,0:T(8,128)(2,1)} %bitcast.38, f32[1,4096]{1,0:T(1,128)} %bitcast.49, bf16[4096,1024]{1,0:T(8,128)(2,1)} %bitcast.40), custom_call_target="tpu_custom_call" | custom-call | flops 17179869184 | bytes 33554432 | tf_op jit(solution)/shard_map/inner_forward/pallas_call | solution.py:188
  328.5 34.9 %inner_backward.1 = (bf16[1024,1024]{1,0:T(8,128)(2,1)}, f32[1024,1024]{1,0:T(8,128)}, bf16[1024,1024]{1,0:T(8,128)(2,1)}, f32[1,4096]{1,0:T(1,128)}, f32[1,1024...) custom-call(f32[1024,1024]{1,0:T(8,128)} %get-tuple-element.32.normal, ...), custom_call_target="tpu_custom_call" | custom-call | flops 17179869184 | bytes 48234496 | tf_op jit(solution)/shard_map/inner_backward/pallas_call | solution.py:291
  363.5 29.6 %attend_backward.1 = (bf16[1024,1024]{1,0:T(8,128)(2,1)}, bf16[1024,1024]{1,0:T(8,128)(2,1)}, bf16[1024,1024]{1,0:T(8,128)(2,1)}, f32[1,1024]{1,0:T(1,128)}, f32[1,1024]{1,0:T(1,128)}) custom-call(bf16[1024,1024]{1,0:T(8,128)(2,1)} %get-tuple-element.38.branch, bf16[1024,1024]{1,0:T(8,128)(2,1)} %get-tuple-element.53.wo, ...), custom_call_target="tpu_custom_call" | custom-call | flops 19327352832 | bytes 37748736 | tf_op jit(solution)/shard_map/attend_backward/pallas_call | solution.py:375
  393.1 0.7 constant_dynamic-update-slice_fusion.6
  393.8 0.7 constant_dynamic-update-slice_fusion.5
  394.6 39.6 %psum.7 = f32[10240]{0:T(1024)S(1)} all-reduce(f32[10240]{0:T(1024)S(1)} %bitcast.47), channel_id=1, replica_groups=mesh['quad'=4,'core'=2,'tp'=4] {'quad','core','tp'}, use_global_device_ids=true, to_apply=%region_0.0 | all-reduce | flops 10240 | bytes 81920 | tf_op jit(solution)/shard_map/psum | solution.py:502
  434.2 0.6 fusion
  435.4 12.5 %tokens_backward.1 = f32[1024,1024]{1,0:T(8,128)} custom-call(f32[1024,1024]{1,0:T(8,128)} %get-tuple-element.37.first, bf16[1024,1024]{1,0:T(8,128)(2,1)} %get-tuple-element.43.dq, bf16[1024,1024]{1,0:T(8,128)(2,1)} %get-tuple-element.44.dk, bf16[1024,1024]{1,0:T(8,128)(2,1)} %get-tuple-element.45.dv, bf16[1024,1024]{1,0:T(8,128)(2,1)} %get-tuple-element.56.wq, ...), custom_call_target="tpu_custom_call" | custom-call | flops 6442450944 | bytes 20971520 | tf_op jit(solution)/shard_map/tokens_backward/pallas_call | solution.py:416
  (31 shorter events, 0.9 us)
Async XLA Ops:
  7.2 1.6 copy-start
  7.2 5.8 %copy-start.3 = (s32[2,512]{1,0:T(2,128)S(1)}, s32[2,512]{1,0:T(2,128)}, u32[]{:S(2)}) copy-start(s32[2,512]{1,0:T(2,128)} %param.19) | copy-start | bytes 12292
  7.2 7.5 %copy-start.4 = (f32[1024]{0:T(1024)S(1)}, f32[1024]{0:T(1024)}, u32[]{:S(2)}) copy-start(f32[1024]{0:T(1024)} %param.30) | copy-start | bytes 12292
  7.2 84.0 %all-gather.8.cloned.1.call-start = ((), (), s32[]{:S(2)}) async-start(), calls=%async_computation.1 | async-start | bytes 8650752 | tf_op jit(solution)/shard_map/all_gather | solution.py:442
  9.5 160.7 %all-gather.10.cloned.1.call-start = ((), (), s32[]{:S(2)}) async-start(), calls=%async_computation.2 | async-start | bytes 8650752 | tf_op jit(solution)/shard_map/all_gather | solution.py:446
  11.3 238.6 %all-gather.6.cloned.1.call-start = ((), (), s32[]{:S(2)}) async-start(), calls=%async_computation | async-start | bytes 8650752 | tf_op jit(solution)/shard_map/all_gather | solution.py:439
  363.5 31.1 %copy-start.8 = (f32[1,1024]{1,0:T(1,128)S(1)}, f32[1,1024]{1,0:T(1,128)}, u32[]{:S(2)}) copy-start(f32[1,1024]{1,0:T(1,128)} %get-tuple-element.48) | copy-start | bytes 12292
  363.5 31.1 %copy-start.7 = (f32[1,1024]{1,0:T(1,128)S(1)}, f32[1,1024]{1,0:T(1,128)}, u32[]{:S(2)}) copy-start(f32[1,1024]{1,0:T(1,128)} %get-tuple-element.49) | copy-start | bytes 12292
  363.5 31.1 %copy-start.6 = (f32[1,1024]{1,0:T(1,128)S(1)}, f32[1,1024]{1,0:T(1,128)}, u32[]{:S(2)}) copy-start(f32[1,1024]{1,0:T(1,128)} %get-tuple-element.50) | copy-start | bytes 12292
  363.5 31.1 %copy-start.5 = (f32[1,1024]{1,0:T(1,128)S(1)}, f32[1,1024]{1,0:T(1,128)}, u32[]{:S(2)}) copy-start(f32[1,1024]{1,0:T(1,128)} %get-tuple-element.51) | copy-start | bytes 12292
  363.5 31.1 %copy-start.2 = (f32[1,4096]{1,0:T(1,128)S(1)}, f32[1,4096]{1,0:T(1,128)}, u32[]{:S(2)}) copy-start(f32[1,4096]{1,0:T(1,128)} %get-tuple-element.52) | copy-start | bytes 49156
  435.4 12.5 %copy-start.1 = (bf16[1024,1024]{1,0:T(8,128)(2,1)S(1)}, bf16[1024,1024]{1,0:T(8,128)(2,1)}, u32[]{:S(2)}) copy-start(bf16[1024,1024]{1,0:T(8,128)(2,1)} %param.29) | copy-start | bytes 6291460
Sparse Core Ops, SparseCore 0:
  11.0 80.2 all-gather.7
  94.2 76.0 all-gather.9
  173.9 76.0 all-gather.5
